TPU v7x, 32 devices: a whole 2x2x4 slice. The times are simulated.
32 devices in a mesh: group: 8 (over z, y), chain: 4 (over x, core).
Axes of the slice: x: 2, y: 2, z: 4, core: 2. Of those that a mesh axis runs over, the one named last changes fastest.
Arguments:
- query_gates: bfloat16 [4096, 2048], P(('group', 'chain')), may hold values from -6 to 6
- address_vectors: bfloat16 [4096, 2048], P(('group', 'chain')), may hold values from -6 to 6
- payload_vectors: bfloat16 [4096, 2048], P(('group', 'chain')), may hold values from -6 to 6
- unscaled_erase_address: bfloat16 [4096, 2048], P(('group', 'chain')), may hold values from -6 to 6
- adaptive_step_factor: bfloat16 [4096, 2048], P(('group', 'chain')), may hold values from 0 to 1
- fading_exponent: float32 [4096, 2048], P(('group', 'chain')), may hold values from -0.7 to 0
- diagonal_reward: float32 [32, 64], replicated, may hold values from -0.75 to 0.75
- standardize_scale: float32 [2048], replicated, may hold values from 0.5 to 1.5
- standardize_shift: float32 [2048], replicated, may hold values from -3 to 3
Outputs:
- output: bfloat16 [4096, 2048], P(('group', 'chain'))
All inputs are finite; a program needn't handle non-finite values.
Results may differ from a plain program's by a relative error of at most 0.001.
Values sent between devices are 32-bit elements; how exact they have to be, the bound alone decides.
A program may use at most 320 MiB of HBM per device.

v0:
```python
import jax
import jax.numpy as jnp
from jax import lax
from jax.sharding import PartitionSpec as P

DEVICE_SUBSPACES = 32
SUBSPACE_WIDTH = 64
BLOCK = 64


highest = lax.Precision.HIGHEST


def prefix(shard, axis, combine, identity):
    length, place = (lax.axis_size(axis), lax.axis_index(axis))
    everything = lax.all_gather(shard, axis)
    start = jnp.broadcast_to(jnp.asarray(identity, shard.dtype), shard.shape)

    def lap(k, before):
        reached = k < place
        new = combine(before, everything[k])
        return jnp.where(reached, new, before)

    return lax.fori_loop(0, length, lap, start)


def from_root(value, axis, source):
    kept = jnp.where(lax.axis_index(axis) == source, value, 0).astype(value.dtype)
    return lax.psum(kept, axis)


def blockwise(array, blocks):
    shaped = array.astype(jnp.float32).reshape(blocks, BLOCK, DEVICE_SUBSPACES, SUBSPACE_WIDTH)
    return jnp.transpose(shaped, (0, 2, 1, 3))


def products(left, right, mask):
    return jnp.einsum("nhtk,nhsk->nhts", left, right, precision=highest) * mask


def batched_square(matrix, other):
    return jnp.einsum("nhts,nhsu->nhtu", matrix, other, precision=highest)


def unit_lower_inverse(lower_part):
    eye_block = jnp.eye(BLOCK, dtype=jnp.float32)
    inverse = eye_block - lower_part
    power = lower_part
    reach = 1
    while 2 * reach < BLOCK:
        power = batched_square(power, power)
        inverse = batched_square(inverse, eye_block + power)
        reach = 2 * reach
    return inverse


def compose(earlier, later):
    forward = jnp.einsum("hij,hjk->hik", earlier[0], later[0], precision=highest)
    carried = jnp.einsum("hij,hjk->hik", earlier[1], later[0], precision=highest) + later[1]
    return jnp.stack([forward, carried])


def advance(state, inputs):
    (
        kappa_before,
        padded_values,
        recept_through,
        key_tail,
        strength_tail,
        inverse_system,
        key_mix,
        read_key,
        read_strength,
        decay_end,
    ) = inputs
    right = jnp.einsum("htk,hrk->htr", kappa_before, state, precision=highest)
    right = right + jnp.einsum("hts,hsr->htr", key_mix, padded_values, precision=highest)
    removed = jnp.einsum("hts,hsr->htr", inverse_system, right, precision=highest)
    reading = jnp.einsum("htk,hrk->htr", recept_through, state, precision=highest)
    reading = reading + jnp.einsum("hts,hsr->htr", read_key, padded_values, precision=highest)
    reading = reading - jnp.einsum("hts,hsr->htr", read_strength, removed, precision=highest)
    state = state * decay_end[:, None, :]
    state = state + jnp.einsum("hsr,hsk->hrk", padded_values, key_tail, precision=highest)
    state = state - jnp.einsum("hsr,hsk->hrk", removed, strength_tail, precision=highest)
    return (state, reading)


def per_device(
    query_gates,
    address_vectors,
    payload_vectors,
    unscaled_erase_address,
    adaptive_step_factor,
    fading_exponent,
    diagonal_reward,
    standardize_scale,
    standardize_shift,
):
    rows = query_gates.shape[0]
    blocks = rows // BLOCK
    query_gate_vectors = blockwise(query_gates, blocks)
    address_weighted = blockwise(address_vectors, blocks)
    payload_weighted = blockwise(payload_vectors, blocks)
    raw_key = blockwise(unscaled_erase_address, blocks)
    kappa = raw_key * lax.rsqrt(jnp.sum(raw_key * raw_key, axis=-1, keepdims=True) + 1e-06)
    strength = blockwise(adaptive_step_factor, blocks) * kappa
    log_step = blockwise(fading_exponent, blocks)
    cumul = jnp.cumsum(log_step, axis=2)
    ending = cumul[:, :, -1:, :]
    inverse = jnp.exp(-cumul)
    tail_factor = jnp.exp(ending - cumul)
    key_scaled = address_weighted * inverse
    strength_scaled = strength * inverse
    kappa_before = kappa * jnp.exp(cumul - log_step)
    recept_through = query_gate_vectors * jnp.exp(cumul)
    key_tail = address_weighted * tail_factor
    strength_tail = strength * tail_factor
    decay_end = jnp.exp(ending[:, :, 0, :])
    strict_mask = jnp.tril(jnp.ones((BLOCK, BLOCK), jnp.float32), -1)
    inclusive_mask = jnp.tril(jnp.ones((BLOCK, BLOCK), jnp.float32), 0)
    key_mix = products(kappa_before, key_scaled, strict_mask)
    inverse_system = unit_lower_inverse(products(kappa_before, strength_scaled, strict_mask))
    read_key = products(recept_through, key_scaled, inclusive_mask)
    read_strength = products(recept_through, strength_scaled, inclusive_mask)
    padded_values = jnp.concatenate([payload_weighted, jnp.zeros_like(payload_weighted)], axis=-1)
    eye_heads = jnp.broadcast_to(
        jnp.eye(SUBSPACE_WIDTH, dtype=jnp.float32),
        (DEVICE_SUBSPACES, SUBSPACE_WIDTH, SUBSPACE_WIDTH),
    )
    start = jnp.concatenate(
        [jnp.zeros((DEVICE_SUBSPACES, SUBSPACE_WIDTH, SUBSPACE_WIDTH), jnp.float32), eye_heads],
        axis=1,
    )
    final_state, readings = lax.scan(
        advance,
        start,
        (
            kappa_before,
            padded_values,
            recept_through,
            key_tail,
            strength_tail,
            inverse_system,
            key_mix,
            read_key,
            read_strength,
            decay_end,
        ),
    )
    local_mixed = readings[..., :SUBSPACE_WIDTH]
    along = readings[..., SUBSPACE_WIDTH:]
    own = jnp.stack([final_state[:, SUBSPACE_WIDTH:, :], final_state[:, :SUBSPACE_WIDTH, :]])
    identity = jnp.stack(
        [eye_heads, jnp.zeros((DEVICE_SUBSPACES, SUBSPACE_WIDTH, SUBSPACE_WIDTH), jnp.float32)]
    )
    inner = prefix(own, "chain", compose, identity)
    total = compose(inner, own)
    chain_whole = from_root(total, "chain", lax.axis_size("chain") - 1)
    outer = prefix(chain_whole, "group", compose, identity)
    incoming = compose(outer, inner)[1]
    mixed = local_mixed + jnp.einsum("hvk,nhtk->nhtv", incoming, along, precision=highest)
    center = mixed - jnp.mean(mixed, axis=-1, keepdims=True)
    variance = jnp.mean(center * center, axis=-1, keepdims=True)
    standardized_result = center * lax.rsqrt(variance + 0.00064)
    diagonal_extra_term = (
        jnp.sum(
            query_gate_vectors * address_weighted * diagonal_reward[None, :, None, :],
            axis=-1,
            keepdims=True,
        )
        * payload_weighted
    )
    subspace_scale = standardize_scale.reshape(1, DEVICE_SUBSPACES, 1, SUBSPACE_WIDTH)
    subspace_shift = standardize_shift.reshape(1, DEVICE_SUBSPACES, 1, SUBSPACE_WIDTH)
    mixer_result = standardized_result * subspace_scale + subspace_shift + diagonal_extra_term
    mixer_result = jnp.transpose(mixer_result, (0, 2, 1, 3)).reshape(
        rows, DEVICE_SUBSPACES * SUBSPACE_WIDTH
    )
    return mixer_result.astype(jnp.bfloat16)


def solution(mesh):
    placed = (
        P(("group", "chain"), None),
        P(("group", "chain"), None),
        P(("group", "chain"), None),
        P(("group", "chain"), None),
        P(("group", "chain"), None),
        P(("group", "chain"), None),
        P(),
        P(),
        P(),
    )
    return jax.shard_map(
        per_device,
        mesh=mesh,
        in_specs=placed,
        out_specs=P(("group", "chain"), None),
        check_vma=False,
    )
```

profile of v0, /device:TPU:25, one launch (start us, length us, event | category | flops | bytes accessed | tf_op | source)
XLA Modules:
  0.0 892.5 jit_solution(14871629146047119274)
XLA Ops:
  8.6 13.9 %fusion.56 = f32[2,32,64,64]{3,1,2,0:T(8,128)S(1)} fusion(f32[2,64,32,64]{3,2,1,0:T(8,128)S(1)} %reshape.93), kind=kOutput, calls=%fused_computation.86 | output fusion | flops 16515072 | bytes 2097152 | tf_op jit(solution)/shard_map/jit(cumsum)/reduce_window_sum | solution.py:108
  35.2 7.3 bitcast_multiply_fusion.5
  53.6 7.4 fusion.84
  61.0 7.2 fusion.90
  68.3 7.4 fusion.87
  111.8 46.7 %while.38 = (s32[]{:T(128)}, f32[32,128,64]{1,2,0:T(8,128)S(1)}, f32[2,32,64,128]{3,2,1,0:T(8,128)}, f32[2,32,64]{2,1,0:T(8,128)S(1)}, f32[2,32,64,128]{3,2,1,0:...) while((s32[]{:T(128)}, f32[32,128,64]{1,2,0:T(8,128)S(1)}, ...), condition=%wide.region_3.4_spmd, body=%wide.region_2.3_spmd.sunk | while | flops 1612185600 | bytes 61370712 | solution.py:134
  163.8 58.0 %all-gather.6.cloned.1.call-done = f32[8,32,64,64]{3,2,1,0:T(8,128)} async-done(((f32[2,32,64,64]{3,2,1,0:T(8,128)}), f32[8,32,64,64]{3,2,1,0:T(8,128)}) %all-gather.6.cloned.1.call-update) | async-done | bytes 4194320 | tf_op jit(solution)/shard_map/all_gather | solution.py:16
  221.8 104.9 %while.39 = (s32[]{:T(128)}, f32[2,32,64,64]{3,2,1,0:T(8,128)}, s32[]{:T(128)}, f32[4,2,32,64,64]{4,3,2,1,0:T(8,128)}, s32[]{:T(128)}, /*index=5*/s32[]{:T(128)}, s32[]{}) while((s32[]{:T(128)}, f32[2,32,64,64]{3,2,1,0:T(8,128)}, s32[]{:T(128)}, f32[4,2,32,64,64]{4,3,2,1,0:T(8,128)}, s32[]{:T(128)}, /*index=5*/s32[]{:T(128)}, s32[]{}) %tuple.101), condition=%wide.region_5.6_spmd, body=%wide.region_4.5_spmd.sunk | while | flops 201981952 | bytes 26216064 | solution.py:24
  221.8 8.9 copy.128
  247.6 8.9 copy.128
  274.0 8.9 copy.128
  300.4 8.9 copy.128
  334.2 51.6 %all-reduce.5.cloned.1.call-done = f32[1,2,32,64,64]{4,3,2,1,0:T(8,128)} async-done(((f32[1,2,32,64,64]{4,3,2,1,0:T(8,128)}), f32[1,2,32,64,64]{4,3,2,1,0:T(8,128)}) %all-reduce.5.cloned.1.call-update) | async-done | bytes 1048592 | tf_op jit(solution)/shard_map/psum | solution.py:29
  393.4 220.9 %all-gather.4.cloned.1.call-done = f32[8,2,32,64,64]{4,3,2,1,0:T(8,128)} async-done(((f32[1,2,32,64,64]{4,3,2,1,0:T(8,128)}), f32[8,2,32,64,64]{4,3,2,1,0:T(8,128)}) %all-gather.4.cloned.1.call-update) | async-done | bytes 8388624 | tf_op jit(solution)/shard_map/all_gather | solution.py:16
  614.2 254.5 %while.40 = (s32[]{:T(128)}, f32[2,32,64,64]{3,2,1,0:T(8,128)S(1)}, s32[]{:T(128)}, f32[8,2,32,64,64]{4,3,2,1,0:T(8,128)}, s32[]{:T(128)}, /*index=5*/s32[]{:T(128)}, s32[]{}) while((s32[]{:T(128)}, f32[2,32,64,64]{3,2,1,0:T(8,128)S(1)}, s32[]{:T(128)}, f32[8,2,32,64,64]{4,3,2,1,0:T(8,128)}, s32[]{:T(128)}, /*index=5*/s32[]{:T(128)}, s32[]{}) %tuple.92), condition=%wide.region_8.9_spmd, body=%wide.region_7.8_spmd.sunk | while | flops 201981952 | bytes 30410340 | solution.py:24
  614.2 17.5 %copy.131 = f32[8,2,32,64,64]{3,4,2,1,0:T(8,128)} copy(f32[8,2,32,64,64]{4,3,2,1,0:T(8,128)} %get-tuple-element.569) | data formatting | bytes 16777216 | tf_op jit(solution)/shard_map
  645.9 17.5 %copy.131 = f32[8,2,32,64,64]{3,4,2,1,0:T(8,128)} copy(f32[8,2,32,64,64]{4,3,2,1,0:T(8,128)} %get-tuple-element.569) | data formatting | bytes 16777216 | tf_op jit(solution)/shard_map
  677.5 17.5 %copy.131 = f32[8,2,32,64,64]{3,4,2,1,0:T(8,128)} copy(f32[8,2,32,64,64]{4,3,2,1,0:T(8,128)} %get-tuple-element.569) | data formatting | bytes 16777216 | tf_op jit(solution)/shard_map
  709.2 17.5 %copy.131 = f32[8,2,32,64,64]{3,4,2,1,0:T(8,128)} copy(f32[8,2,32,64,64]{4,3,2,1,0:T(8,128)} %get-tuple-element.569) | data formatting | bytes 16777216 | tf_op jit(solution)/shard_map
  740.8 17.5 %copy.131 = f32[8,2,32,64,64]{3,4,2,1,0:T(8,128)} copy(f32[8,2,32,64,64]{4,3,2,1,0:T(8,128)} %get-tuple-element.569) | data formatting | bytes 16777216 | tf_op jit(solution)/shard_map
  772.5 17.5 %copy.131 = f32[8,2,32,64,64]{3,4,2,1,0:T(8,128)} copy(f32[8,2,32,64,64]{4,3,2,1,0:T(8,128)} %get-tuple-element.569) | data formatting | bytes 16777216 | tf_op jit(solution)/shard_map
  804.1 17.5 %copy.131 = f32[8,2,32,64,64]{3,4,2,1,0:T(8,128)} copy(f32[8,2,32,64,64]{4,3,2,1,0:T(8,128)} %get-tuple-element.569) | data formatting | bytes 16777216 | tf_op jit(solution)/shard_map
  836.4 17.5 %copy.131 = f32[8,2,32,64,64]{3,4,2,1,0:T(8,128)} copy(f32[8,2,32,64,64]{4,3,2,1,0:T(8,128)} %get-tuple-element.569) | data formatting | bytes 16777216 | tf_op jit(solution)/shard_map
  871.4 8.5 fusion.123
  (212 shorter events, 319.8 us)
Async XLA Ops:
  6.5 215.3 %all-gather.6.cloned.1.call-start = ((), (), s32[]{:S(2)}) async-start(), calls=%async_computation.2 | async-start | bytes 10485760 | tf_op jit(solution)/shard_map/all_gather | solution.py:16
  8.6 15.3 %copy-start.15 = (bf16[128,2048]{1,0:T(8,128)(2,1)S(1)}, bf16[128,2048]{1,0:T(8,128)(2,1)}, u32[]{:S(2)}) copy-start(bf16[128,2048]{1,0:T(8,128)(2,1)} %param.18) | copy-start | bytes 1572868
  23.8 4.6 copy-start.16
  26.1 4.6 copy-start.17
  30.7 4.5 copy-start.21
  98.0 3.5 copy-start.19
  115.2 3.8 copy-start.8
  120.6 2.6 copy-start.7
  126.0 2.6 copy-start.3
  130.2 2.6 copy-start.4
  138.3 3.8 copy-start.8
  143.7 2.6 copy-start.7
  149.1 2.6 copy-start.3
  153.3 2.6 copy-start.4
  162.0 223.8 %all-reduce.5.cloned.1.call-start = ((), (), s32[]{:S(2)}) async-start(), calls=%async_computation | async-start | bytes 4194304 | tf_op jit(solution)/shard_map/psum | solution.py:29
  230.8 3.8 copy-start
  256.5 3.8 copy-start
  282.9 3.8 copy-start
  309.3 3.8 copy-start
  326.8 2.8 copy-start.1
  334.1 280.1 %all-gather.4.cloned.1.call-start = ((), (), s32[]{:S(2)}) async-start(), calls=%async_computation.1 | async-start | bytes 18874368 | tf_op jit(solution)/shard_map/all_gather | solution.py:16
  389.2 4.0 copy-start.20
  389.2 4.0 copy-start.22
  389.2 4.1 copy-start.23
  (13 other events, 24.0 us)
Sparse Core Ops, SparseCore 0:
  162.1 59.6 all-gather.5
  334.3 51.4 all-reduce.4
  388.2 226.0 all-gather.3
where the time goes:
time: 909 us; the launch traced here: 892 us
  waiting for transfers between devices  331 us (36%)
  local copies, waits for them, and re-layouts  280 us (31%)
  matrix products  199 us (22%)
  other arithmetic  68.6 us (8%)
  between operations  13.6 us (1%)
    all_gather x2, waiting for transfers between devices, prefix(): everything = lax.all_gather(shard, axis)  279 us
    another operation x36, local copies, waits for them, and re-layouts  229 us
    psum x1, waiting for transfers between devices, from_root(): return lax.psum(kept, axis)  51.6 us
    dot_general x13, matrix products, compose(): jnp.einsum('hij,hjk->hik', earlier[0], later[0], precision=highest)  50.7 us
    dot_general x14, matrix products, compose(): jnp.einsum('hij,hjk->hik', earlier[1], later[0], precision=highest)  47.2 us
    select_n x12, other arithmetic, lap(): return jnp.where(reached, new, before)  40.2 us
    dot_general x10, matrix products, batched_square(): return jnp.einsum('nhts,nhsu->nhtu', matrix, other, precision=highest)  30.1 us
    dot_general x4, matrix products, products(): return jnp.einsum('nhtk,nhsk->nhts', left, right, precision=highest) * mask  27.9 us
  transfers between devices with their start and end apart: 3, of which 3 were waited for; matrix products, arithmetic and copies ran while one was open for 1% of the time, Pallas kernels for 0%

commit v1 on v0

v1 whole, which is shorter than its diff:
```python
import functools

import jax
import jax.numpy as jnp
from jax import lax
from jax.experimental import pallas as pl
from jax.experimental.pallas import tpu as pltpu
from jax.sharding import PartitionSpec as P

HEADS = 32
WIDTH = 64
PAIRS = 2
f32 = jnp.float32
bf16 = jnp.bfloat16
NN = ((1,), (0,))
NT = ((1,), (1,))
TN = ((0,), (0,))
MESH = pl.DeviceIdType.MESH


def split(x):
    hi = x.astype(bf16)
    return hi, (x - hi.astype(f32)).astype(bf16)


def dot(a, b, dims=NN):
    return lax.dot_general(a, b, (dims, ((), ())), preferred_element_type=f32)


def cat(parts, axis):
    return jnp.concatenate(parts, axis=axis)


def dot3(a, b):
    ah, al = split(a)
    bh, bl = split(b)
    n = b.shape[1]
    right = cat([cat([bh, bl], 1), cat([bh, jnp.zeros_like(bl)], 1)], 0)
    r = dot(cat([ah, al], 1), right)
    return r[:, :n] + r[:, n:]


def column(row):
    return jnp.broadcast_to(row, (8, row.shape[1])).T[:, 0:1]


def local_kernel(q_ref, k_ref, v_ref, e_ref, a_ref, f_ref, u_ref, map_ref, local_ref, along_ref, extra_ref):
    T = q_ref.shape[0]
    row = lax.broadcasted_iota(jnp.int32, (T, T), 0)
    col = lax.broadcasted_iota(jnp.int32, (T, T), 1)
    strict = row < col
    through = row <= col
    top_mask = cat([strict.astype(f32), through.astype(f32)], 1) > 0.5
    differ = row ^ col
    tri = through.astype(bf16)
    tri2 = cat([tri, tri], 0)
    eye = (row == col).astype(f32)
    heads = range(2 * PAIRS)

    kb, rt, ks, ss, vs, kb_abs, rt_abs, kt, st, last = ([] for _ in range(10))
    for p in range(PAIRS):
        lanes = slice(2 * WIDTH * p, 2 * WIDTH * (p + 1))
        q, k, v, e, a = (ref[:, lanes].astype(f32).T for ref in (q_ref, k_ref, v_ref, e_ref, a_ref))
        f = f_ref[:, lanes].T
        u = column(u_ref[:, lanes])
        fh = f.astype(bf16)
        rest = f - fh.astype(f32)
        fm = rest.astype(bf16)
        fl = (rest - fm.astype(f32)).astype(bf16)
        c = dot(cat([fh, fm], 1), tri2) + dot(fl, tri)
        end = c[:, T - 1 : T]
        mid = 0.5 * end
        e_in = jnp.exp(c - mid)
        e_before = jnp.exp(c - f - mid)
        e_inv = jnp.exp(mid - c)
        g = jnp.exp(mid)
        final = jnp.exp(end)
        qku = q * k * u
        for i in range(2):
            r = slice(WIDTH * i, WIDTH * (i + 1))
            kap = e[r] * lax.rsqrt(jnp.sum(e[r] * e[r], axis=0, keepdims=True) + 1e-06)
            stren = a[r] * kap
            kb.append(kap * e_before[r])
            rt.append(q[r] * e_in[r])
            ks.append(k[r] * e_inv[r])
            ss.append(stren * e_inv[r])
            kb_abs.append(kb[-1] * g[r])
            rt_abs.append(rt[-1] * g[r])
            kt.append(ks[-1] * g[r])
            st.append(ss[-1] * g[r])
            last.append(final[r])
            vs.append(v[r].astype(bf16))
            extra_ref[2 * p + i] = jnp.sum(qku[r], axis=0, keepdims=True) * v[r]

    mixes = []
    for h in heads:
        lh, ll = split(cat([ks[h], ss[h]], 1))
        rh, rl = split(cat([kb[h], rt[h]], 1))
        mix = cat([lh, ll], 0).T
        mixes.append(dot(cat([mix, mix], 1), cat([rh, rh, rl, rl], 0)))
    lower = [jnp.where(strict, m[T:, :T], 0.0) for m in mixes]
    read_strength = [jnp.where(through, m[T:, T:], 0.0) for m in mixes]
    values = []
    for h in heads:
        th, tl = split(jnp.where(top_mask, mixes[h][:T], 0.0))
        values.append(dot(cat([vs[h], vs[h]], 1), cat([th, tl], 0)))
    inverse = [eye - jnp.where(differ == 1, low, 0.0) for low in lower]
    bit = 1
    while (2 << bit) <= T:
        here = (differ >> bit) == 1
        step = [dot3(inverse[h], jnp.where(here, lower[h], 0.0)) for h in heads]
        inverse = [inverse[h] - dot3(step[h], inverse[h]) for h in heads]
        bit += 1
    removed = [dot3(cat([values[h][:, :T], kb_abs[h]], 0), inverse[h]) for h in heads]
    read = [dot3(removed[h], read_strength[h]) for h in heads]
    krow = lax.broadcasted_iota(jnp.int32, (WIDTH, 2 * WIDTH), 0)
    kcol = lax.broadcasted_iota(jnp.int32, (WIDTH, 2 * WIDTH), 1)
    diagonal = kcol == krow + WIDTH
    for h in heads:
        local_ref[h] = values[h][:, T:] - read[h][:WIDTH]
        along_ref[h] = rt_abs[h] - read[h][WIDTH:]
        sh, sl = split(st[h])
        kh, kl = split(kt[h])
        wh, wl = split(removed[h])
        vpad = cat([vs[h], jnp.zeros_like(vs[h])], 0)
        gain = dot(cat([kh, kl], 1), cat([vpad, vpad], 1), NT)
        loss = dot(cat([sh, sl], 1), cat([wh, wh], 1), NT) + dot(sh, wl, NT)
        map_ref[h] = gain - loss + jnp.where(diagonal, last[h], 0.0)


def scan_kernel(axes, map_ref, state_ref, inbox, outbox, send1, recv1, send2, recv2):
    (outer_axis, outer), (inner_axis, inner) = axes
    total = outer * inner
    owners = min(total, HEADS)
    share = HEADS // owners
    stride = total // owners
    me = lax.axis_index(outer_axis) * inner + lax.axis_index(inner_axis)
    mine = me // stride
    half = WIDTH // 2

    def place(d):
        return (d // inner, lax.rem(d, inner))

    def when(condition, body):
        if condition is True:
            body()
        else:
            pl.when(condition)(body)

    own = True if stride == 1 else lax.rem(me, stride) == 0

    barrier = pltpu.get_barrier_semaphore()

    def greet_owner(j, _):
        when(j * stride != me, lambda: pl.semaphore_signal(barrier, inc=1, device_id=place(j * stride), device_id_type=MESH))
        return 0

    def greet_rest(d, _):
        when(lax.rem(d, stride) != 0, lambda: pl.semaphore_signal(barrier, inc=1, device_id=place(d), device_id_type=MESH))
        return 0

    lax.fori_loop(0, owners, greet_owner, 0)
    if stride == 1:
        pl.semaphore_wait(barrier, total - 1)
    else:

        def greet():
            lax.fori_loop(0, total, greet_rest, 0)
            pl.semaphore_wait(barrier, total - 1)

        when(own, greet)
        when(lax.rem(me, stride) != 0, lambda: pl.semaphore_wait(barrier, owners))

    def to_owner(j):
        return pltpu.make_async_remote_copy(
            src_ref=map_ref.at[pl.ds(j * share, share)],
            dst_ref=inbox.at[me],
            send_sem=send1.at[j],
            recv_sem=recv1.at[me],
            device_id=place(j * stride),
            device_id_type=MESH,
        )

    def from_device(d):
        return pltpu.make_async_remote_copy(
            src_ref=map_ref.at[pl.ds(0, share)],
            dst_ref=inbox.at[d],
            send_sem=send1.at[0],
            recv_sem=recv1.at[d],
            device_id=place(d),
            device_id_type=MESH,
        )

    def to_device(d):
        return pltpu.make_async_remote_copy(
            src_ref=outbox.at[d],
            dst_ref=state_ref.at[pl.ds(mine * share, share)],
            send_sem=send2.at[d],
            recv_sem=recv2.at[mine],
            device_id=place(d),
            device_id_type=MESH,
        )

    def from_owner(j):
        return pltpu.make_async_remote_copy(
            src_ref=outbox.at[0],
            dst_ref=state_ref.at[pl.ds(j * share, share)],
            send_sem=send2.at[0],
            recv_sem=recv2.at[j],
            device_id=place(j * stride),
            device_id_type=MESH,
        )

    def send_map(n, _):
        j = lax.rem(mine + n, owners)
        when(j * stride != me, lambda: to_owner(j).start())
        return 0

    lax.fori_loop(0, owners, send_map, 0)

    def scan():
        for i in range(share):
            inbox[me, i] = map_ref[mine * share + i]

        def advance(d, states):
            when(d != me, lambda: from_device(d).wait_recv())
            new = []
            for i, s in enumerate(states):
                outbox[d, i] = cat([s[:half], s[half:]], 1)
                m = inbox[d, i]
                mh, ml = split(m)
                sh, sl = split(s)
                zero = jnp.zeros_like(sh)
                moved = dot(cat([mh, ml], 1), cat([zero, sh, zero, sh], 0)) + dot(mh, cat([zero, sl], 0))
                new.append(m[:, :WIDTH] + moved)
            return tuple(new)

        lax.fori_loop(0, total, advance, tuple(jnp.zeros((WIDTH, WIDTH), f32) for _ in range(share)))
        for i in range(share):
            state_ref[mine * share + i] = outbox[me, i]

        def send_state(n, _):
            to_device(lax.rem(me + n, total)).start()
            return 0

        lax.fori_loop(1, total, send_state, 0)

    when(own, scan)

    def finish_owner(j, _):
        def body():
            from_owner(j).wait_recv()
            to_owner(j).wait_send()

        when(j * stride != me, body)
        return 0

    lax.fori_loop(0, owners, finish_owner, 0)

    def finish_states():
        def finish_device(n, _):
            to_device(lax.rem(me + n, total)).wait_send()
            return 0

        lax.fori_loop(1, total, finish_device, 0)

    when(own, finish_states)


def final_kernel(state_ref, local_ref, along_ref, extra_ref, scale_ref, shift_ref, out_ref):
    half = WIDTH // 2
    for p in range(PAIRS):
        lanes = slice(2 * WIDTH * p, 2 * WIDTH * (p + 1))
        parts = []
        for h in (2 * p, 2 * p + 1):
            packed = state_ref[h]
            s = cat([packed[:, :WIDTH], packed[:, WIDTH:]], 0)
            sh, sl = split(s)
            ah, al = split(along_ref[h])
            mixed = local_ref[h] + dot(cat([sh, sh, sl], 0), cat([ah, al, ah], 0), TN)
            center = mixed - jnp.mean(mixed, axis=0, keepdims=True)
            variance = jnp.mean(center * center, axis=0, keepdims=True)
            parts.append(center * lax.rsqrt(variance + 0.00064))
        normed = cat(parts, 0) * column(scale_ref[:, lanes]) + column(shift_ref[:, lanes])
        normed = normed + cat([extra_ref[2 * p], extra_ref[2 * p + 1]], 0)
        out_ref[:, lanes] = normed.T.astype(out_ref.dtype)


def per_device(axes, q, k, v, e, a, f, reward, scale, shift):
    rows, columns = q.shape
    total = axes[0][1] * axes[1][1]
    owners = min(total, HEADS)
    share = HEADS // owners
    lanes = 2 * WIDTH * PAIRS
    steps = columns // lanes
    tokens = pl.BlockSpec((rows, lanes), lambda i: (0, i))
    vector = pl.BlockSpec((1, lanes), lambda i: (0, i))
    def per_head(n, m):
        return pl.BlockSpec((2 * PAIRS, n, m), lambda i: (i, 0, 0))

    maps, local, along, extra = pl.pallas_call(
        local_kernel,
        grid=(steps,),
        in_specs=[tokens] * 6 + [vector],
        out_specs=[per_head(WIDTH, 2 * WIDTH)] + [per_head(WIDTH, rows)] * 3,
        out_shape=[jax.ShapeDtypeStruct((HEADS, WIDTH, 2 * WIDTH), f32)]
        + [jax.ShapeDtypeStruct((HEADS, WIDTH, rows), f32)] * 3,
        compiler_params=pltpu.CompilerParams(vmem_limit_bytes=48 * 2**20),
        name="local",
    )(q, k, v, e, a, f, reward.reshape(1, columns))

    states = pl.pallas_call(
        functools.partial(scan_kernel, axes),
        in_specs=[pl.BlockSpec(memory_space=pltpu.VMEM)],
        out_specs=pl.BlockSpec(memory_space=pltpu.VMEM),
        out_shape=jax.ShapeDtypeStruct((HEADS, WIDTH // 2, 2 * WIDTH), f32),
        scratch_shapes=[
            pltpu.VMEM((total, share, WIDTH, 2 * WIDTH), f32),
            pltpu.VMEM((total, share, WIDTH // 2, 2 * WIDTH), f32),
            pltpu.SemaphoreType.DMA((owners,)),
            pltpu.SemaphoreType.DMA((total,)),
            pltpu.SemaphoreType.DMA((total,)),
            pltpu.SemaphoreType.DMA((owners,)),
        ],
        compiler_params=pltpu.CompilerParams(
            collective_id=0, has_side_effects=True, vmem_limit_bytes=48 * 2**20
        ),
        name="scan",
    )(maps)

    return pl.pallas_call(
        final_kernel,
        grid=(steps,),
        in_specs=[per_head(WIDTH // 2, 2 * WIDTH)] + [per_head(WIDTH, rows)] * 3 + [vector] * 2,
        out_specs=tokens,
        out_shape=jax.ShapeDtypeStruct((rows, columns), bf16),
        compiler_params=pltpu.CompilerParams(vmem_limit_bytes=48 * 2**20),
        name="final",
    )(states, local, along, extra, scale.reshape(1, columns), shift.reshape(1, columns))


def solution(mesh):
    axes = tuple((name, mesh.shape[name]) for name in mesh.axis_names)
    placed = (P(axes_names(mesh), None),) * 6 + (P(),) * 3
    return jax.shard_map(
        functools.partial(per_device, axes),
        mesh=mesh,
        in_specs=placed,
        out_specs=P(axes_names(mesh), None),
        check_vma=False,
    )


def axes_names(mesh):
    return tuple(mesh.axis_names)
```

time: 909 us -> 88.3 us (0.10)
  the two profiles are of different devices: /device:TPU:25 before, /device:TPU:21 now
where the time goes in v1:
time: 88.3 us; the launch traced here: 87.9 us
  Pallas kernels  81.8 us (93%)
  local copies, waits for them, and re-layouts  6.01 us (7%)
    pallas_call x1, Pallas kernels, per_device(): pl.pallas_call(functools.partial(scan_kernel, axes), in_specs=[pl.BlockSp...  51 us
    pallas_call x1, Pallas kernels, per_device(): pl.pallas_call(local_kernel, grid=(steps,), in_specs=[tokens] * 6 + [vect...  25 us
    pallas_call x1, Pallas kernels, per_device(): pl.pallas_call(final_kernel, grid=(steps,), in_specs=[per_head(WIDTH // 2...  5.87 us
    unnamed x16, local copies, waits for them, and re-layouts  5.22 us

profile of v1, /device:TPU:21, one launch (start us, length us, event | category | flops | bytes accessed | tf_op | source)
XLA Modules:
  0.0 87.9 jit_solution(5658970674769382150)
XLA Ops:
  0.0 0.8 reshape.9.u_ref
  0.8 0.0 copy-start.1
  0.8 1.0 %copy-done.1 = bf16[128,2048]{1,0:T(8,128)(2,1)S(1)} copy-done((bf16[128,2048]{1,0:T(8,128)(2,1)S(1)}, bf16[128,2048]{1,0:T(8,128)(2,1)}, u32[]{:S(2)}) %copy-start.1) | copy-done | bytes 524312
  1.8 0.0 copy-start.2
  1.8 1.0 %copy-done.2 = bf16[128,2048]{1,0:T(8,128)(2,1)S(1)} copy-done((bf16[128,2048]{1,0:T(8,128)(2,1)S(1)}, bf16[128,2048]{1,0:T(8,128)(2,1)}, u32[]{:S(2)}) %copy-start.2) | copy-done | bytes 524312
  2.9 0.0 copy-start.3
  2.9 1.0 %copy-done.3 = bf16[128,2048]{1,0:T(8,128)(2,1)S(1)} copy-done((bf16[128,2048]{1,0:T(8,128)(2,1)S(1)}, bf16[128,2048]{1,0:T(8,128)(2,1)}, u32[]{:S(2)}) %copy-start.3) | copy-done | bytes 524312
  3.9 0.0 copy-start.4
  3.9 1.0 %copy-done.4 = bf16[128,2048]{1,0:T(8,128)(2,1)S(1)} copy-done((bf16[128,2048]{1,0:T(8,128)(2,1)S(1)}, bf16[128,2048]{1,0:T(8,128)(2,1)}, u32[]{:S(2)}) %copy-start.4) | copy-done | bytes 524312
  5.0 0.0 copy-start.5
  5.0 1.0 %copy-done.5 = bf16[128,2048]{1,0:T(8,128)(2,1)S(1)} copy-done((bf16[128,2048]{1,0:T(8,128)(2,1)S(1)}, bf16[128,2048]{1,0:T(8,128)(2,1)}, u32[]{:S(2)}) %copy-start.5) | copy-done | bytes 524312
  6.0 25.0 %local.1 = (f32[32,64,128]{2,1,0:T(8,128)S(1)}, f32[32,64,128]{2,1,0:T(8,128)S(1)}, f32[32,64,128]{2,1,0:T(8,128)S(1)}, f32[32,64,128]{2,1,0:T(8,128)}) custom-call(bf16[128,2048]{1,0:T(8,128)(2,1)S(1)} %copy-done.1, bf16[128,2048]{1,0:T(8,128)(2,1)S(1)} %copy-done.2, bf16[128,2048]{1,0:T(8,128)(2,1)S(1)} %copy-done.3, bf16[128,2048]{1,0:T(8,128)(2,1)S(1)} %copy-done.4, ...), custom_call_target="tpu_custom_call" | custom-call | tf_op jit(solution)/shard_map/local/pallas_call | solution.py:301
  31.0 0.0 copy-start
  31.0 0.0 copy-start.6
  31.0 0.0 copy-start.7
  31.0 51.0 %scan.1.state_ref = f32[32,32,128]{2,1,0:T(8,128)S(1)} custom-call(f32[32,64,128]{2,1,0:T(8,128)S(1)} %get-tuple-element.9.map_ref), custom_call_target="tpu_custom_call" | custom-call | tf_op jit(solution)/shard_map/scan/pallas_call | solution.py:312
  82.0 0.0 copy-done
  82.0 0.0 copy-done.6
  82.0 0.0 copy-done.7
  82.0 5.9 %final.1 = bf16[128,2048]{1,0:T(8,128)(2,1)} custom-call(f32[32,32,128]{2,1,0:T(8,128)S(1)} %scan.1.state_ref, f32[32,64,128]{2,1,0:T(8,128)S(1)} %get-tuple-element.10.local_ref, f32[32,64,128]{2,1,0:T(8,128)S(1)} %get-tuple-element.11.along_ref, f32[32,64,128]{2,1,0:T(8,128)S(1)} %copy-done, f32[1,2048]{1,0:T(1,128)S(1)} %bitcast.2, f32[1,2048]{1,0:T(1,128)S(1)} %bitcast.3), custom_call_target="tpu_custom_call" | custom-call | tf_op jit(solution)/shard_map/final/pallas_call | solution.py:331
Async XLA Ops:
  0.8 1.0 %copy-start.1 = (bf16[128,2048]{1,0:T(8,128)(2,1)S(1)}, bf16[128,2048]{1,0:T(8,128)(2,1)}, u32[]{:S(2)}) copy-start(bf16[128,2048]{1,0:T(8,128)(2,1)} %q_ref.1) | copy-start | bytes 1572868
  1.8 1.0 %copy-start.2 = (bf16[128,2048]{1,0:T(8,128)(2,1)S(1)}, bf16[128,2048]{1,0:T(8,128)(2,1)}, u32[]{:S(2)}) copy-start(bf16[128,2048]{1,0:T(8,128)(2,1)} %k_ref.1) | copy-start | bytes 1572868
  2.9 1.0 %copy-start.3 = (bf16[128,2048]{1,0:T(8,128)(2,1)S(1)}, bf16[128,2048]{1,0:T(8,128)(2,1)}, u32[]{:S(2)}) copy-start(bf16[128,2048]{1,0:T(8,128)(2,1)} %v_ref.1) | copy-start | bytes 1572868
  3.9 1.0 %copy-start.4 = (bf16[128,2048]{1,0:T(8,128)(2,1)S(1)}, bf16[128,2048]{1,0:T(8,128)(2,1)}, u32[]{:S(2)}) copy-start(bf16[128,2048]{1,0:T(8,128)(2,1)} %e_ref.1) | copy-start | bytes 1572868
  5.0 1.0 %copy-start.5 = (bf16[128,2048]{1,0:T(8,128)(2,1)S(1)}, bf16[128,2048]{1,0:T(8,128)(2,1)}, u32[]{:S(2)}) copy-start(bf16[128,2048]{1,0:T(8,128)(2,1)} %a_ref.1) | copy-start | bytes 1572868
  31.0 51.0 %copy-start = (f32[32,64,128]{2,1,0:T(8,128)S(1)}, f32[32,64,128]{2,1,0:T(8,128)}, u32[]{:S(2)}) copy-start(f32[32,64,128]{2,1,0:T(8,128)} %get-tuple-element.12.extra_ref) | copy-start | bytes 3145732
  31.0 51.0 %copy-start.6 = (f32[2048]{0:T(1024)S(1)}, f32[2048]{0:T(1024)}, u32[]{:S(2)}) copy-start(f32[2048]{0:T(1024)} %param.16) | copy-start | bytes 24580
  31.0 51.0 %copy-start.7 = (f32[2048]{0:T(1024)S(1)}, f32[2048]{0:T(1024)}, u32[]{:S(2)}) copy-start(f32[2048]{0:T(1024)} %param.17) | copy-start | bytes 24580

commit v2 on v1

--- a/solution.py
+++ b/solution.py
@@ -128,7 +128,7 @@
         map_ref[h] = gain - loss + jnp.where(diagonal, last[h], 0.0)
 
 
-def scan_kernel(axes, map_ref, state_ref, inbox, outbox, send1, recv1, send2, recv2):
+def scan_kernel(axes, map_ref, state_ref, inbox, outbox, prefix, send1, recv1, send2, recv2):
     (outer_axis, outer), (inner_axis, inner) = axes
     total = outer * inner
     owners = min(total, HEADS)
@@ -222,20 +222,55 @@
         for i in range(share):
             inbox[me, i] = map_ref[mine * share + i]
 
-        def advance(d, states):
+        def arrive(d, _):
             when(d != me, lambda: from_device(d).wait_recv())
-            new = []
-            for i, s in enumerate(states):
-                outbox[d, i] = cat([s[:half], s[half:]], 1)
-                m = inbox[d, i]
-                mh, ml = split(m)
-                sh, sl = split(s)
-                zero = jnp.zeros_like(sh)
-                moved = dot(cat([mh, ml], 1), cat([zero, sh, zero, sh], 0)) + dot(mh, cat([zero, sl], 0))
-                new.append(m[:, :WIDTH] + moved)
-            return tuple(new)
-
-        lax.fori_loop(0, total, advance, tuple(jnp.zeros((WIDTH, WIDTH), f32) for _ in range(share)))
+            return 0
+
+        lax.fori_loop(0, total, arrive, 0)
+        segments = 4 if total % 4 == 0 else 1
+        length = total // segments
+        krow = lax.broadcasted_iota(jnp.int32, (WIDTH, 2 * WIDTH), 0)
+        kcol = lax.broadcasted_iota(jnp.int32, (WIDTH, 2 * WIDTH), 1)
+        unit = (kcol == krow + WIDTH).astype(f32)
+        offset = kcol < WIDTH
+
+        def right_side(s):
+            sh, sl = split(s)
+            zero = jnp.zeros_like(sh)
+            return cat([zero, sh, zero, sh], 0), cat([zero, sl], 0)
+
+        def apply(m, right):
+            mh, ml = split(m)
+            return dot(cat([mh, ml], 1), right[0]) + dot(mh, right[1])
+
+        for i in range(share):
+
+            def advance(t, before):
+                after = []
+                for g in range(segments):
+                    d = g * length + t
+                    prefix[d] = before[g]
+                    m = inbox[d, i]
+                    after.append(apply(m, right_side(before[g])) + jnp.where(offset, m, 0.0))
+                return tuple(after)
+
+            ends = lax.fori_loop(0, length, advance, (unit,) * segments)
+            s = jnp.zeros((WIDTH, WIDTH), f32)
+            rights = []
+            for g in range(segments):
+                rights.append(right_side(s))
+                s = apply(ends[g], rights[g]) + ends[g][:, :WIDTH]
+
+            def place_states(t, _):
+                for g in range(segments):
+                    d = g * length + t
+                    m = prefix[d]
+                    s = apply(m, rights[g]) + m[:, :WIDTH]
+                    outbox[d, i] = cat([s[:half], s[half:]], 1)
+                return 0
+
+            lax.fori_loop(0, length, place_states, 0)
+
         for i in range(share):
             state_ref[mine * share + i] = outbox[me, i]
 
@@ -305,7 +340,7 @@
         out_specs=[per_head(WIDTH, 2 * WIDTH)] + [per_head(WIDTH, rows)] * 3,
         out_shape=[jax.ShapeDtypeStruct((HEADS, WIDTH, 2 * WIDTH), f32)]
         + [jax.ShapeDtypeStruct((HEADS, WIDTH, rows), f32)] * 3,
-        compiler_params=pltpu.CompilerParams(vmem_limit_bytes=48 * 2**20),
+        compiler_params=pltpu.CompilerParams(vmem_limit_bytes=62 * 2**20),
         name="local",
     )(q, k, v, e, a, f, reward.reshape(1, columns))
 
@@ -317,6 +352,7 @@
         scratch_shapes=[
             pltpu.VMEM((total, share, WIDTH, 2 * WIDTH), f32),
             pltpu.VMEM((total, share, WIDTH // 2, 2 * WIDTH), f32),
+            pltpu.VMEM((total, WIDTH, 2 * WIDTH), f32),
             pltpu.SemaphoreType.DMA((owners,)),
             pltpu.SemaphoreType.DMA((total,)),
             pltpu.SemaphoreType.DMA((total,)),
@@ -334,7 +370,7 @@
         in_specs=[per_head(WIDTH // 2, 2 * WIDTH)] + [per_head(WIDTH, rows)] * 3 + [vector] * 2,
         out_specs=tokens,
         out_shape=jax.ShapeDtypeStruct((rows, columns), bf16),
-        compiler_params=pltpu.CompilerParams(vmem_limit_bytes=48 * 2**20),
+        compiler_params=pltpu.CompilerParams(vmem_limit_bytes=62 * 2**20),
         name="final",
     )(states, local, along, extra, scale.reshape(1, columns), shift.reshape(1, columns))
 

time: 88.3 us -> 83.1 us (0.941)
  the two profiles are of different devices: /device:TPU:21 before, /device:TPU:25 now
where the time goes in v2:
time: 83.1 us; the launch traced here: 82 us
  Pallas kernels  78.6 us (95%)
  local copies, waits for them, and re-layouts  3.4 us (4%)
    pallas_call x1, Pallas kernels, per_device(): pl.pallas_call(functools.partial(scan_kernel, axes), in_specs=[pl.BlockSp...  45.2 us
    pallas_call x1, Pallas kernels, per_device(): pl.pallas_call(local_kernel, grid=(steps,), in_specs=[tokens] * 6 + [vect...  25 us
    pallas_call x1, Pallas kernels, per_device(): pl.pallas_call(final_kernel, grid=(steps,), in_specs=[per_head(WIDTH // 2...  8.3 us
    unnamed x4, local copies, waits for them, and re-layouts  2 us

profile of v2, /device:TPU:25, one launch (start us, length us, event | category | flops | bytes accessed | tf_op | source)
XLA Modules:
  0.0 82.0 jit_solution(6493946046612517094)
XLA Ops:
  0.0 1.4 %reshape.9.u_ref = f32[1,2048]{1,0:T(1,128)} reshape(f32[32,64]{1,0:T(8,128)} %param.15) | data formatting | bytes 16384 | tf_op jit(solution)/shard_map/reshape | solution.py:345
  1.4 25.0 %local.1 = (f32[32,64,128]{2,1,0:T(8,128)}, f32[32,64,128]{2,1,0:T(8,128)}, f32[32,64,128]{2,1,0:T(8,128)}, f32[32,64,128]{2,1,0:T(8,128)}) custom-call(bf16[128,2048]{1,0:T(8,128)(2,1)} %q_ref.1, bf16[128,2048]{1,0:T(8,128)(2,1)} %k_ref.1, bf16[128,2048]{1,0:T(8,128)(2,1)} %v_ref.1, bf16[128,2048]{1,0:T(8,128)(2,1)} %e_ref.1, bf16[128,2048]{1,0:T(8,128)(2,1)} %a_ref.1, ...), custom_call_target="tpu_custom_call" | custom-call | tf_op jit(solution)/shard_map/local/pallas_call | solution.py:336
  26.4 0.0 copy-start.1
  26.5 1.2 %copy-done.1 = f32[32,64,128]{2,1,0:T(8,128)S(1)} copy-done((f32[32,64,128]{2,1,0:T(8,128)S(1)}, f32[32,64,128]{2,1,0:T(8,128)}, u32[]{:S(2)}) %copy-start.1) | copy-done | bytes 1048600
  27.7 45.2 %scan.1.state_ref = f32[32,32,128]{2,1,0:T(8,128)S(1)} custom-call(f32[32,64,128]{2,1,0:T(8,128)S(1)} %copy-done.1), custom_call_target="tpu_custom_call" | custom-call | tf_op jit(solution)/shard_map/scan/pallas_call | solution.py:347
  72.9 0.0 copy-start
  72.9 0.8 copy-done
  73.7 8.3 %final.1 = bf16[128,2048]{1,0:T(8,128)(2,1)} custom-call(f32[32,32,128]{2,1,0:T(8,128)} %copy-done, f32[32,64,128]{2,1,0:T(8,128)} %get-tuple-element.10.local_ref, f32[32,64,128]{2,1,0:T(8,128)} %get-tuple-element.11.along_ref, f32[32,64,128]{2,1,0:T(8,128)} %get-tuple-element.12.extra_ref, f32[1,2048]{1,0:T(1,128)} %bitcast.2, f32[1,2048]{1,0:T(1,128)} %bitcast.3), custom_call_target="tpu_custom_call" | custom-call | tf_op jit(solution)/shard_map/final/pallas_call | solution.py:367
Async XLA Ops:
  26.4 1.2 %copy-start.1 = (f32[32,64,128]{2,1,0:T(8,128)S(1)}, f32[32,64,128]{2,1,0:T(8,128)}, u32[]{:S(2)}) copy-start(f32[32,64,128]{2,1,0:T(8,128)} %get-tuple-element.9.map_ref) | copy-start | bytes 3145732
  72.9 0.8 copy-start

commit v3 on v2

--- a/solution.py
+++ b/solution.py
@@ -9,7 +9,7 @@
 
 HEADS = 32
 WIDTH = 64
-PAIRS = 2
+PAIRS = 4
 f32 = jnp.float32
 bf16 = jnp.bfloat16
 NN = ((1,), (0,))

time: 83.1 us -> 74.8 us (0.900)
  Pallas kernels: 78.6 us -> 70.5 us
    pallas_call x1, Pallas kernels: 25 us -> 17.8 us  [per_device(): pl.pallas_call(local_kernel, grid=(steps,), in_specs=[tokens] * 6 + [vect...]
where the time goes in v3:
time: 74.8 us; the launch traced here: 73.9 us
  Pallas kernels  70.5 us (94%)
  local copies, waits for them, and re-layouts  3.4 us (5%)
    pallas_call x1, Pallas kernels, per_device(): pl.pallas_call(functools.partial(scan_kernel, axes), in_specs=[pl.BlockSp...  45.2 us
    pallas_call x1, Pallas kernels, per_device(): pl.pallas_call(local_kernel, grid=(steps,), in_specs=[tokens] * 6 + [vect...  17.8 us
    pallas_call x1, Pallas kernels, per_device(): pl.pallas_call(final_kernel, grid=(steps,), in_specs=[per_head(WIDTH // 2...  7.5 us
    unnamed x4, local copies, waits for them, and re-layouts  2 us

profile of v3, /device:TPU:25, one launch (start us, length us, event | category | flops | bytes accessed | tf_op | source)
XLA Modules:
  0.0 73.9 jit_solution(6594508368233206389)
XLA Ops:
  0.0 1.4 %reshape.9.u_ref = f32[1,2048]{1,0:T(1,128)} reshape(f32[32,64]{1,0:T(8,128)} %param.15) | data formatting | bytes 16384 | tf_op jit(solution)/shard_map/reshape | solution.py:345
  1.4 17.8 %local.1 = (f32[32,64,128]{2,1,0:T(8,128)}, f32[32,64,128]{2,1,0:T(8,128)}, f32[32,64,128]{2,1,0:T(8,128)}, f32[32,64,128]{2,1,0:T(8,128)}) custom-call(bf16[128,2048]{1,0:T(8,128)(2,1)} %q_ref.1, bf16[128,2048]{1,0:T(8,128)(2,1)} %k_ref.1, bf16[128,2048]{1,0:T(8,128)(2,1)} %v_ref.1, bf16[128,2048]{1,0:T(8,128)(2,1)} %e_ref.1, bf16[128,2048]{1,0:T(8,128)(2,1)} %a_ref.1, ...), custom_call_target="tpu_custom_call" | custom-call | tf_op jit(solution)/shard_map/local/pallas_call | solution.py:336
  19.2 0.0 copy-start.1
  19.2 1.2 %copy-done.1 = f32[32,64,128]{2,1,0:T(8,128)S(1)} copy-done((f32[32,64,128]{2,1,0:T(8,128)S(1)}, f32[32,64,128]{2,1,0:T(8,128)}, u32[]{:S(2)}) %copy-start.1) | copy-done | bytes 1048600
  20.4 45.2 %scan.1.state_ref = f32[32,32,128]{2,1,0:T(8,128)S(1)} custom-call(f32[32,64,128]{2,1,0:T(8,128)S(1)} %copy-done.1), custom_call_target="tpu_custom_call" | custom-call | tf_op jit(solution)/shard_map/scan/pallas_call | solution.py:347
  65.6 0.0 copy-start
  65.6 0.8 %copy-done = f32[32,32,128]{2,1,0:T(8,128)} copy-done((f32[32,32,128]{2,1,0:T(8,128)}, f32[32,32,128]{2,1,0:T(8,128)S(1)}, u32[]{:S(2)}) %copy-start) | copy-done | bytes 524312
  66.4 7.5 %final.1 = bf16[128,2048]{1,0:T(8,128)(2,1)} custom-call(f32[32,32,128]{2,1,0:T(8,128)} %copy-done, f32[32,64,128]{2,1,0:T(8,128)} %get-tuple-element.10.local_ref, f32[32,64,128]{2,1,0:T(8,128)} %get-tuple-element.11.along_ref, f32[32,64,128]{2,1,0:T(8,128)} %get-tuple-element.12.extra_ref, f32[1,2048]{1,0:T(1,128)} %bitcast.2, f32[1,2048]{1,0:T(1,128)} %bitcast.3), custom_call_target="tpu_custom_call" | custom-call | tf_op jit(solution)/shard_map/final/pallas_call | solution.py:367
Async XLA Ops:
  19.2 1.2 %copy-start.1 = (f32[32,64,128]{2,1,0:T(8,128)S(1)}, f32[32,64,128]{2,1,0:T(8,128)}, u32[]{:S(2)}) copy-start(f32[32,64,128]{2,1,0:T(8,128)} %get-tuple-element.9.map_ref) | copy-start | bytes 3145732
  65.6 0.8 %copy-start = (f32[32,32,128]{2,1,0:T(8,128)}, f32[32,32,128]{2,1,0:T(8,128)S(1)}, u32[]{:S(2)}) copy-start(f32[32,32,128]{2,1,0:T(8,128)S(1)} %scan.1.state_ref) | copy-start | bytes 1572868

commit v4 on v1

--- a/solution.py
+++ b/solution.py
@@ -9,7 +9,7 @@
 
 HEADS = 32
 WIDTH = 64
-PAIRS = 2
+PAIRS = 4
 f32 = jnp.float32
 bf16 = jnp.bfloat16
 NN = ((1,), (0,))
@@ -128,76 +128,69 @@
         map_ref[h] = gain - loss + jnp.where(diagonal, last[h], 0.0)
 
 
-def scan_kernel(axes, map_ref, state_ref, inbox, outbox, send1, recv1, send2, recv2):
+def slab_of(total):
+    return min(8, total // 2)
+
+
+def scan_kernel(
+    axes, map_ref, state_ref, inbox, outbox, prefix, carry_in, carry_out, send1, recv1, send2, recv2, send3, recv3
+):
     (outer_axis, outer), (inner_axis, inner) = axes
     total = outer * inner
-    owners = min(total, HEADS)
-    share = HEADS // owners
-    stride = total // owners
+    slab = slab_of(total)
+    slabs = total // slab
+    share = HEADS // slab
     me = lax.axis_index(outer_axis) * inner + lax.axis_index(inner_axis)
-    mine = me // stride
+    z = me // slab
+    base = z * slab
+    pos = me - base
     half = WIDTH // 2
 
     def place(d):
         return (d // inner, lax.rem(d, inner))
 
-    def when(condition, body):
-        if condition is True:
-            body()
-        else:
-            pl.when(condition)(body)
-
-    own = True if stride == 1 else lax.rem(me, stride) == 0
-
     barrier = pltpu.get_barrier_semaphore()
 
-    def greet_owner(j, _):
-        when(j * stride != me, lambda: pl.semaphore_signal(barrier, inc=1, device_id=place(j * stride), device_id_type=MESH))
-        return 0
-
-    def greet_rest(d, _):
-        when(lax.rem(d, stride) != 0, lambda: pl.semaphore_signal(barrier, inc=1, device_id=place(d), device_id_type=MESH))
-        return 0
-
-    lax.fori_loop(0, owners, greet_owner, 0)
-    if stride == 1:
-        pl.semaphore_wait(barrier, total - 1)
-    else:
-
-        def greet():
-            lax.fori_loop(0, total, greet_rest, 0)
-            pl.semaphore_wait(barrier, total - 1)
-
-        when(own, greet)
-        when(lax.rem(me, stride) != 0, lambda: pl.semaphore_wait(barrier, owners))
+    def greet(d):
+        pl.semaphore_signal(barrier, inc=1, device_id=place(d), device_id_type=MESH)
+
+    def greet_member(n, _):
+        greet(base + lax.rem(pos + n, slab))
+        return 0
+
+    lax.fori_loop(1, slab, greet_member, 0)
+    pl.when(z > 0)(lambda: greet(me - slab))
+    pl.when(z < slabs - 1)(lambda: greet(me + slab))
+    neighbours = (z + slabs - 1) // slabs + (2 * slabs - 2 - z) // slabs
+    pl.semaphore_wait(barrier, slab - 1 + neighbours)
 
     def to_owner(j):
         return pltpu.make_async_remote_copy(
             src_ref=map_ref.at[pl.ds(j * share, share)],
-            dst_ref=inbox.at[me],
+            dst_ref=inbox.at[pos],
             send_sem=send1.at[j],
-            recv_sem=recv1.at[me],
-            device_id=place(j * stride),
-            device_id_type=MESH,
-        )
-
-    def from_device(d):
+            recv_sem=recv1.at[pos],
+            device_id=place(base + j),
+            device_id_type=MESH,
+        )
+
+    def from_member(d):
         return pltpu.make_async_remote_copy(
             src_ref=map_ref.at[pl.ds(0, share)],
             dst_ref=inbox.at[d],
             send_sem=send1.at[0],
             recv_sem=recv1.at[d],
-            device_id=place(d),
-            device_id_type=MESH,
-        )
-
-    def to_device(d):
+            device_id=place(base + d),
+            device_id_type=MESH,
+        )
+
+    def to_member(d):
         return pltpu.make_async_remote_copy(
             src_ref=outbox.at[d],
-            dst_ref=state_ref.at[pl.ds(mine * share, share)],
+            dst_ref=state_ref.at[pl.ds(pos * share, share)],
             send_sem=send2.at[d],
-            recv_sem=recv2.at[mine],
-            device_id=place(d),
+            recv_sem=recv2.at[pos],
+            device_id=place(base + d),
             device_id_type=MESH,
         )
 
@@ -207,64 +200,100 @@
             dst_ref=state_ref.at[pl.ds(j * share, share)],
             send_sem=send2.at[0],
             recv_sem=recv2.at[j],
-            device_id=place(j * stride),
+            device_id=place(base + j),
+            device_id_type=MESH,
+        )
+
+    def to_slab(d):
+        return pltpu.make_async_remote_copy(
+            src_ref=carry_out,
+            dst_ref=carry_in,
+            send_sem=send3,
+            recv_sem=recv3,
+            device_id=place(d),
             device_id_type=MESH,
         )
 
     def send_map(n, _):
-        j = lax.rem(mine + n, owners)
-        when(j * stride != me, lambda: to_owner(j).start())
-        return 0
-
-    lax.fori_loop(0, owners, send_map, 0)
-
-    def scan():
+        to_owner(lax.rem(pos + n, slab)).start()
+        return 0
+
+    lax.fori_loop(1, slab, send_map, 0)
+    for i in range(share):
+        inbox[pos, i] = map_ref[pos * share + i]
+
+    def arrive(n, _):
+        from_member(lax.rem(pos + n, slab)).wait_recv()
+        return 0
+
+    lax.fori_loop(1, slab, arrive, 0)
+    krow = lax.broadcasted_iota(jnp.int32, (WIDTH, 2 * WIDTH), 0)
+    kcol = lax.broadcasted_iota(jnp.int32, (WIDTH, 2 * WIDTH), 1)
+    unit = (kcol == krow + WIDTH).astype(f32)
+    offset = kcol < WIDTH
+
+    def right_side(s):
+        sh, sl = split(s)
+        zero = jnp.zeros_like(sh)
+        return cat([zero, sh, zero, sh], 0), cat([zero, sl], 0)
+
+    def apply(m, right):
+        mh, ml = split(m)
+        return dot(cat([mh, ml], 1), right[0]) + dot(mh, right[1])
+
+    def pack(s):
+        return cat([s[:half], s[half:]], 1)
+
+    def advance(t, before):
+        after = []
         for i in range(share):
-            inbox[me, i] = map_ref[mine * share + i]
-
-        def advance(d, states):
-            when(d != me, lambda: from_device(d).wait_recv())
-            new = []
-            for i, s in enumerate(states):
-                outbox[d, i] = cat([s[:half], s[half:]], 1)
-                m = inbox[d, i]
-                mh, ml = split(m)
-                sh, sl = split(s)
-                zero = jnp.zeros_like(sh)
-                moved = dot(cat([mh, ml], 1), cat([zero, sh, zero, sh], 0)) + dot(mh, cat([zero, sl], 0))
-                new.append(m[:, :WIDTH] + moved)
-            return tuple(new)
-
-        lax.fori_loop(0, total, advance, tuple(jnp.zeros((WIDTH, WIDTH), f32) for _ in range(share)))
+            prefix[t, i] = before[i]
+            m = inbox[t, i]
+            after.append(apply(m, right_side(before[i])) + jnp.where(offset, m, 0.0))
+        return tuple(after)
+
+    ends = lax.fori_loop(0, slab, advance, (unit,) * share)
+
+    @pl.when(z == 0)
+    def _():
+        carry_in[...] = jnp.zeros_like(carry_in)
+
+    pl.when(z > 0)(lambda: to_slab(me - slab).wait_recv())
+    rights = []
+    for i in range(share):
+        packed = carry_in[i]
+        rights.append(right_side(cat([packed[:, :WIDTH], packed[:, WIDTH:]], 0)))
+
+    @pl.when(z < slabs - 1)
+    def _():
         for i in range(share):
-            state_ref[mine * share + i] = outbox[me, i]
-
-        def send_state(n, _):
-            to_device(lax.rem(me + n, total)).start()
-            return 0
-
-        lax.fori_loop(1, total, send_state, 0)
-
-    when(own, scan)
-
-    def finish_owner(j, _):
-        def body():
-            from_owner(j).wait_recv()
-            to_owner(j).wait_send()
-
-        when(j * stride != me, body)
-        return 0
-
-    lax.fori_loop(0, owners, finish_owner, 0)
-
-    def finish_states():
-        def finish_device(n, _):
-            to_device(lax.rem(me + n, total)).wait_send()
-            return 0
-
-        lax.fori_loop(1, total, finish_device, 0)
-
-    when(own, finish_states)
+            carry_out[i] = pack(apply(ends[i], rights[i]) + ends[i][:, :WIDTH])
+        to_slab(me + slab).start()
+
+    def state(t, i):
+        m = prefix[t, i]
+        return pack(apply(m, rights[i]) + m[:, :WIDTH])
+
+    def send_state(n, _):
+        t = lax.rem(pos + n, slab)
+        for i in range(share):
+            outbox[t, i] = state(t, i)
+        to_member(t).start()
+        return 0
+
+    lax.fori_loop(1, slab, send_state, 0)
+    for i in range(share):
+        state_ref[pos * share + i] = state(pos, i)
+
+    def finish(n, _):
+        j = lax.rem(pos + n, slab)
+        from_owner(j).wait_recv()
+        to_owner(j).wait_send()
+        to_member(j).wait_send()
+        return 0
+
+    lax.fori_loop(1, slab, finish, 0)
+    pl.when(z < slabs - 1)(lambda: to_slab(me + slab).wait_send())
 
 
 def final_kernel(state_ref, local_ref, along_ref, extra_ref, scale_ref, shift_ref, out_ref):
@@ -289,8 +318,8 @@
 def per_device(axes, q, k, v, e, a, f, reward, scale, shift):
     rows, columns = q.shape
     total = axes[0][1] * axes[1][1]
-    owners = min(total, HEADS)
-    share = HEADS // owners
+    slab = slab_of(total)
+    share = HEADS // slab
     lanes = 2 * WIDTH * PAIRS
     steps = columns // lanes
     tokens = pl.BlockSpec((rows, lanes), lambda i: (0, i))
@@ -305,7 +334,7 @@
         out_specs=[per_head(WIDTH, 2 * WIDTH)] + [per_head(WIDTH, rows)] * 3,
         out_shape=[jax.ShapeDtypeStruct((HEADS, WIDTH, 2 * WIDTH), f32)]
         + [jax.ShapeDtypeStruct((HEADS, WIDTH, rows), f32)] * 3,
-        compiler_params=pltpu.CompilerParams(vmem_limit_bytes=48 * 2**20),
+        compiler_params=pltpu.CompilerParams(vmem_limit_bytes=62 * 2**20),
         name="local",
     )(q, k, v, e, a, f, reward.reshape(1, columns))
 
@@ -315,13 +344,14 @@
         out_specs=pl.BlockSpec(memory_space=pltpu.VMEM),
         out_shape=jax.ShapeDtypeStruct((HEADS, WIDTH // 2, 2 * WIDTH), f32),
         scratch_shapes=[
-            pltpu.VMEM((total, share, WIDTH, 2 * WIDTH), f32),
-            pltpu.VMEM((total, share, WIDTH // 2, 2 * WIDTH), f32),
-            pltpu.SemaphoreType.DMA((owners,)),
-            pltpu.SemaphoreType.DMA((total,)),
-            pltpu.SemaphoreType.DMA((total,)),
-            pltpu.SemaphoreType.DMA((owners,)),
-        ],
+            pltpu.VMEM((slab, share, WIDTH, 2 * WIDTH), f32),
+            pltpu.VMEM((slab, share, WIDTH // 2, 2 * WIDTH), f32),
+            pltpu.VMEM((slab, share, WIDTH, 2 * WIDTH), f32),
+            pltpu.VMEM((share, WIDTH // 2, 2 * WIDTH), f32),
+            pltpu.VMEM((share, WIDTH // 2, 2 * WIDTH), f32),
+        ]
+        + [pltpu.SemaphoreType.DMA((slab,))] * 4
+        + [pltpu.SemaphoreType.DMA] * 2,
         compiler_params=pltpu.CompilerParams(
             collective_id=0, has_side_effects=True, vmem_limit_bytes=48 * 2**20
         ),
@@ -334,7 +364,7 @@
         in_specs=[per_head(WIDTH // 2, 2 * WIDTH)] + [per_head(WIDTH, rows)] * 3 + [vector] * 2,
         out_specs=tokens,
         out_shape=jax.ShapeDtypeStruct((rows, columns), bf16),
-        compiler_params=pltpu.CompilerParams(vmem_limit_bytes=48 * 2**20),
+        compiler_params=pltpu.CompilerParams(vmem_limit_bytes=62 * 2**20),
         name="final",
     )(states, local, along, extra, scale.reshape(1, columns), shift.reshape(1, columns))
 

time: 88.3 us -> 62.3 us (0.71)
  the two profiles are of different devices: /device:TPU:21 before, /device:TPU:25 now
where the time goes in v4:
time: 62.3 us; the launch traced here: 62.1 us
  Pallas kernels  58.6 us (94%)
  local copies, waits for them, and re-layouts  3.4 us (5%)
    pallas_call x1, Pallas kernels, per_device(): pl.pallas_call(functools.partial(scan_kernel, axes), in_specs=[pl.BlockSp...  33.4 us
    pallas_call x1, Pallas kernels, per_device(): pl.pallas_call(local_kernel, grid=(steps,), in_specs=[tokens] * 6 + [vect...  17.8 us
    pallas_call x1, Pallas kernels, per_device(): pl.pallas_call(final_kernel, grid=(steps,), in_specs=[per_head(WIDTH // 2...  7.5 us
    unnamed x4, local copies, waits for them, and re-layouts  2 us
    reshape x1, local copies, waits for them, and re-layouts, per_device(): reward.reshape(1, columns)  1.39 us

profile of v4, /device:TPU:25, one launch (start us, length us, event | category | flops | bytes accessed | tf_op | source)
XLA Modules:
  0.0 62.1 jit_solution(11644672529635440948)
XLA Ops:
  0.0 1.4 %reshape.9.u_ref = f32[1,2048]{1,0:T(1,128)} reshape(f32[32,64]{1,0:T(8,128)} %param.15) | data formatting | bytes 16384 | tf_op jit(solution)/shard_map/reshape | solution.py:339
  1.4 17.8 %local.1 = (f32[32,64,128]{2,1,0:T(8,128)}, f32[32,64,128]{2,1,0:T(8,128)}, f32[32,64,128]{2,1,0:T(8,128)}, f32[32,64,128]{2,1,0:T(8,128)}) custom-call(bf16[128,2048]{1,0:T(8,128)(2,1)} %q_ref.1, bf16[128,2048]{1,0:T(8,128)(2,1)} %k_ref.1, bf16[128,2048]{1,0:T(8,128)(2,1)} %v_ref.1, bf16[128,2048]{1,0:T(8,128)(2,1)} %e_ref.1, bf16[128,2048]{1,0:T(8,128)(2,1)} %a_ref.1, ...), custom_call_target="tpu_custom_call" | custom-call | tf_op jit(solution)/shard_map/local/pallas_call | solution.py:330
  19.2 0.0 copy-start.1
  19.2 1.2 %copy-done.1 = f32[32,64,128]{2,1,0:T(8,128)S(1)} copy-done((f32[32,64,128]{2,1,0:T(8,128)S(1)}, f32[32,64,128]{2,1,0:T(8,128)}, u32[]{:S(2)}) %copy-start.1) | copy-done | bytes 1048600
  20.4 33.4 %scan.1.state_ref = f32[32,32,128]{2,1,0:T(8,128)S(1)} custom-call(f32[32,64,128]{2,1,0:T(8,128)S(1)} %copy-done.1), custom_call_target="tpu_custom_call" | custom-call | tf_op jit(solution)/shard_map/scan/pallas_call | solution.py:341
  53.8 0.0 copy-start
  53.8 0.8 %copy-done = f32[32,32,128]{2,1,0:T(8,128)} copy-done((f32[32,32,128]{2,1,0:T(8,128)}, f32[32,32,128]{2,1,0:T(8,128)S(1)}, u32[]{:S(2)}) %copy-start) | copy-done | bytes 524312
  54.6 7.5 %final.1 = bf16[128,2048]{1,0:T(8,128)(2,1)} custom-call(f32[32,32,128]{2,1,0:T(8,128)} %copy-done, f32[32,64,128]{2,1,0:T(8,128)} %get-tuple-element.10.local_ref, f32[32,64,128]{2,1,0:T(8,128)} %get-tuple-element.11.along_ref, f32[32,64,128]{2,1,0:T(8,128)} %get-tuple-element.12.extra_ref, f32[1,2048]{1,0:T(1,128)} %bitcast.2, f32[1,2048]{1,0:T(1,128)} %bitcast.3), custom_call_target="tpu_custom_call" | custom-call | tf_op jit(solution)/shard_map/final/pallas_call | solution.py:361
Async XLA Ops:
  19.2 1.2 %copy-start.1 = (f32[32,64,128]{2,1,0:T(8,128)S(1)}, f32[32,64,128]{2,1,0:T(8,128)}, u32[]{:S(2)}) copy-start(f32[32,64,128]{2,1,0:T(8,128)} %get-tuple-element.9.map_ref) | copy-start | bytes 3145732
  53.8 0.8 %copy-start = (f32[32,32,128]{2,1,0:T(8,128)}, f32[32,32,128]{2,1,0:T(8,128)S(1)}, u32[]{:S(2)}) copy-start(f32[32,32,128]{2,1,0:T(8,128)S(1)} %scan.1.state_ref) | copy-start | bytes 1572868

commit v5 on v4

--- a/solution.py
+++ b/solution.py
@@ -9,7 +9,7 @@
 
 HEADS = 32
 WIDTH = 64
-PAIRS = 4
+PAIRS = 8
 f32 = jnp.float32
 bf16 = jnp.bfloat16
 NN = ((1,), (0,))

time: 62.3 us -> 62.3 us (level)
  no operation moved by 1% of the time
where the time goes in v5:
time: 62.3 us; the launch traced here: 62 us
  Pallas kernels  58.6 us (94%)
  local copies, waits for them, and re-layouts  3.4 us (5%)
    pallas_call x1, Pallas kernels, per_device(): pl.pallas_call(functools.partial(scan_kernel, axes), in_specs=[pl.BlockSp...  33.4 us
    pallas_call x1, Pallas kernels, per_device(): pl.pallas_call(local_kernel, grid=(steps,), in_specs=[tokens] * 6 + [vect...  18.3 us
    pallas_call x1, Pallas kernels, per_device(): pl.pallas_call(final_kernel, grid=(steps,), in_specs=[per_head(WIDTH // 2...  6.9 us
    unnamed x4, local copies, waits for them, and re-layouts  2 us
    reshape x1, local copies, waits for them, and re-layouts, per_device(): reward.reshape(1, columns)  1.39 us

profile of v5, /device:TPU:25, one launch (start us, length us, event | category | flops | bytes accessed | tf_op | source)
XLA Modules:
  0.0 62.0 jit_solution(501641061131310052)
XLA Ops:
  0.0 1.4 %reshape.9.u_ref = f32[1,2048]{1,0:T(1,128)} reshape(f32[32,64]{1,0:T(8,128)} %param.15) | data formatting | bytes 16384 | tf_op jit(solution)/shard_map/reshape | solution.py:339
  1.4 18.3 %local.1 = (f32[32,64,128]{2,1,0:T(8,128)}, f32[32,64,128]{2,1,0:T(8,128)}, f32[32,64,128]{2,1,0:T(8,128)}, f32[32,64,128]{2,1,0:T(8,128)}) custom-call(bf16[128,2048]{1,0:T(8,128)(2,1)} %q_ref.1, bf16[128,2048]{1,0:T(8,128)(2,1)} %k_ref.1, bf16[128,2048]{1,0:T(8,128)(2,1)} %v_ref.1, bf16[128,2048]{1,0:T(8,128)(2,1)} %e_ref.1, bf16[128,2048]{1,0:T(8,128)(2,1)} %a_ref.1, ...), custom_call_target="tpu_custom_call" | custom-call | tf_op jit(solution)/shard_map/local/pallas_call | solution.py:330
  19.7 0.0 copy-start.1
  19.7 1.2 %copy-done.1 = f32[32,64,128]{2,1,0:T(8,128)S(1)} copy-done((f32[32,64,128]{2,1,0:T(8,128)S(1)}, f32[32,64,128]{2,1,0:T(8,128)}, u32[]{:S(2)}) %copy-start.1) | copy-done | bytes 1048600
  20.9 33.4 %scan.1.state_ref = f32[32,32,128]{2,1,0:T(8,128)S(1)} custom-call(f32[32,64,128]{2,1,0:T(8,128)S(1)} %copy-done.1), custom_call_target="tpu_custom_call" | custom-call | tf_op jit(solution)/shard_map/scan/pallas_call | solution.py:341
  54.3 0.0 copy-start
  54.3 0.8 %copy-done = f32[32,32,128]{2,1,0:T(8,128)} copy-done((f32[32,32,128]{2,1,0:T(8,128)}, f32[32,32,128]{2,1,0:T(8,128)S(1)}, u32[]{:S(2)}) %copy-start) | copy-done | bytes 524312
  55.1 6.9 %final.1 = bf16[128,2048]{1,0:T(8,128)(2,1)} custom-call(f32[32,32,128]{2,1,0:T(8,128)} %copy-done, f32[32,64,128]{2,1,0:T(8,128)} %get-tuple-element.10.local_ref, f32[32,64,128]{2,1,0:T(8,128)} %get-tuple-element.11.along_ref, f32[32,64,128]{2,1,0:T(8,128)} %get-tuple-element.12.extra_ref, f32[1,2048]{1,0:T(1,128)} %bitcast.2, f32[1,2048]{1,0:T(1,128)} %bitcast.3), custom_call_target="tpu_custom_call" | custom-call | tf_op jit(solution)/shard_map/final/pallas_call | solution.py:361
Async XLA Ops:
  19.7 1.2 %copy-start.1 = (f32[32,64,128]{2,1,0:T(8,128)S(1)}, f32[32,64,128]{2,1,0:T(8,128)}, u32[]{:S(2)}) copy-start(f32[32,64,128]{2,1,0:T(8,128)} %get-tuple-element.9.map_ref) | copy-start | bytes 3145732
  54.3 0.8 %copy-start = (f32[32,32,128]{2,1,0:T(8,128)}, f32[32,32,128]{2,1,0:T(8,128)S(1)}, u32[]{:S(2)}) copy-start(f32[32,32,128]{2,1,0:T(8,128)S(1)} %scan.1.state_ref) | copy-start | bytes 1572868
